TPU v7x, 256 devices: a whole 4x4x8 slice. The times are simulated.
256 devices in a mesh: seq: 64 (over x, z, core), ch: 4 (over y).
Axes of the slice: x: 4, y: 4, z: 8, core: 2. Of those that a mesh axis runs over, the one named last changes fastest.
Arguments:
- query_proj: bfloat16 [8192, 2048], P('seq', 'ch'), may hold values from -6 to 6
- key_proj: bfloat16 [8192, 2048], P('seq', 'ch'), may hold values from -6 to 6
- value_proj: bfloat16 [8192, 2048], P('seq', 'ch'), may hold values from -6 to 6
- filters: bfloat16 [8192, 2048], P('seq', 'ch'), may hold values from -1.3 to 1.3
- out_weight: bfloat16 [2048, 4096], P('ch'), may hold values from -0.125 to 0.125
- grad_out: bfloat16 [8192, 4096], P('seq', 'ch'), may hold values from -6 to 6
Outputs:
- output: bfloat16 [8192, 4096], P('seq', 'ch')
- grad_query: bfloat16 [8192, 2048], P('seq', 'ch')
- grad_key: bfloat16 [8192, 2048], P('seq', 'ch')
- grad_value: bfloat16 [8192, 2048], P('seq', 'ch')
- grad_filter: float32 [8192, 2048], P('seq', 'ch')
- grad_weight: float32 [2048, 4096], P('ch', 'seq')
All inputs are finite; a program needn't handle non-finite values.
Results may differ from a plain program's by a relative error of at most 0.02.
Values may be sent and summed in bfloat16 or wider, within the bound.
A program may use at most 128 MiB of HBM per device.

v0:
```python
import functools

import jax
import jax.numpy as jnp
import numpy as np
from jax import lax
from jax.experimental import pallas as pl
from jax.experimental.pallas import tpu as pltpu
from jax.sharding import PartitionSpec as P

F32 = jnp.float32
BF16 = jnp.bfloat16
MESH = pl.DeviceIdType.MESH
GRID = {64: (4, 8, 2), 8: (2, 2, 2)}


def tables(outer, inner):
    length = outer * inner
    i = np.arange(outer)
    j = np.arange(inner)
    first = 2.0 * np.pi * i[:, None] * (i[None, :] + 0.25) / outer
    twist = 2.0 * np.pi * j[None, :] * (i[:, None] + 0.25) / length
    second = 2.0 * np.pi * (j[:, None] * j[None, :] % inner) / inner
    cos, sin = np.cos(second), np.sin(second)
    outer_fwd = np.concatenate([np.cos(first).T, -np.sin(first).T], 0)
    inner_fwd = np.block([[cos, -sin], [sin, cos]])
    outer_bwd = np.concatenate([np.cos(first), -np.sin(first)], 1) / length
    found = (outer_fwd, inner_fwd, inner_fwd.T, outer_bwd, np.cos(twist), np.sin(twist))
    return [t.astype(np.float32) for t in found]


def halves(table):
    high = table.astype(BF16)
    return high, (table - high.astype(F32)).astype(BF16)


def split_wide(real, imag):
    wide = jnp.concatenate([real, imag], axis=1)
    high = wide.astype(BF16)
    low = (wide - high.astype(F32)).astype(BF16)
    return jnp.concatenate([high, low, high], axis=1)


def dot(a, b):
    return jnp.dot(a, b, preferred_element_type=F32)


def kernel(
    sizes,
    q_ref, k_ref, v_ref, f_ref, w_hbm, go_ref,
    fo_in, fi_in, bi_in, bo_in, cos_ref, sin_ref,
    out_ref, gq_ref, gk_ref, gv_ref, gf_ref, gw_ref,
    fo_ref, fi_ref, bi_ref, bo_ref, w_ref, send_a, recv_a, send_b, recv_b, send_c, recv_c, send_d, recv_d,
    wide, spec_g, spec_f, spec_h, zbuf, full, full_t, mix_send, mix_recv,
    grad_recv, part_send, part_own, part_recv, out_send, out_recv, out_own, gm_t, q_t,
    load_sem, send_sem, recv_sem,
):
    nx, nz, ns, ny, rows, scale = sizes
    me = lax.axis_index("seq")
    my = lax.axis_index("ch")
    my_x, my_z, my_k = me // (2 * nz), me // 2 % nz, me % 2
    group = nx * 2
    place = my_x * 2 + my_k
    chans = ns * 8

    def peer(step):
        return lax.rem(me + step, ns)

    def member(step):
        other = lax.rem(place + step, group)
        return other, (other // 2 * nz + my_z) * 2 + other % 2

    load = pltpu.make_async_copy(w_hbm, w_ref, load_sem)
    load.start()

    barrier = pltpu.get_barrier_semaphore()

    def greet(step, carry):
        pl.semaphore_signal(barrier, inc=1, device_id={"seq": peer(step)}, device_id_type=MESH)
        return carry

    lax.fori_loop(1, ns, greet, 0)
    for step in range(1, ny):
        pl.semaphore_signal(barrier, inc=1, device_id={"ch": lax.rem(my + step, ny)}, device_id_type=MESH)

    gated = k_ref[...].astype(F32) * v_ref[...].astype(F32)
    gated_t = gated.T.reshape(ns, 8, rows)
    taps_t = f_ref[...].astype(F32).T.reshape(ns, 8, rows)
    send_a[...] = jnp.concatenate([gated_t, taps_t], axis=1).astype(BF16)
    recv_a[me] = send_a[me]
    full[my] = go_ref[...]
    pl.semaphore_wait(barrier, ns - 1 + ny - 1)

    def exchange(send, recv, index, wide_slots):
        def slot(ref, i, count=1):
            if wide_slots:
                return ref.at[pl.ds(pl.multiple_of(i * 8, 8), 8 * count)]
            return ref.at[pl.ds(i, count)]

        def start(step, carry):
            other = peer(step)
            pltpu.make_async_remote_copy(
                src_ref=slot(send, other), dst_ref=slot(recv, me),
                send_sem=send_sem.at[index], recv_sem=recv_sem.at[index],
                device_id={"seq": other}, device_id_type=MESH,
            ).start()
            return carry

        lax.fori_loop(1, ns, start, 0)
        return pltpu.make_async_remote_copy(
            src_ref=slot(send, 0, ns - 1), dst_ref=slot(recv, 0, ns - 1),
            send_sem=send_sem.at[index], recv_sem=recv_sem.at[index],
            device_id={"seq": peer(1)}, device_id_type=MESH,
        )

    def gather_ch(send, recv, index):
        for step in range(1, ny):
            other = lax.rem(my + step, ny)
            pltpu.make_async_remote_copy(
                src_ref=send(other), dst_ref=recv.at[my],
                send_sem=send_sem.at[index], recv_sem=recv_sem.at[index],
                device_id={"ch": other}, device_id_type=MESH,
            ).start()
        return pltpu.make_async_remote_copy(
            src_ref=recv.at[pl.ds(0, ny - 1)], dst_ref=recv.at[pl.ds(0, ny - 1)],
            send_sem=send_sem.at[index], recv_sem=recv_sem.at[index],
            device_id={"ch": lax.rem(my + 1, ny)}, device_id_type=MESH,
        )

    moved_a = exchange(send_a, recv_a, 0, False)
    moved_full = gather_ch(lambda other: go_ref, full, 1)
    high, low = halves(fo_in[...])
    fo_ref[...] = jnp.concatenate([high, low], axis=1)
    high, low = halves(fi_in[...])
    fi_ref[...] = jnp.concatenate([high, high, low], axis=0)
    high, low = halves(bi_in[...])
    bi_ref[...] = jnp.concatenate([high, high, low], axis=0)
    high, low = halves(bo_in[...])
    bo_ref[...] = jnp.concatenate([high, high, low], axis=1)
    q_t[...] = q_ref[...].astype(F32).T

    def spectra(count, base, spec, spec_base, signals):
        for s in range(0, signals, 2):
            pair = [wide[pl.ds(base + s + u, ns, stride=count), :] for u in range(2)]
            block = jnp.concatenate(pair, axis=1).astype(BF16)
            stage = dot(fo_ref[...], jnp.concatenate([block, block], axis=0))
            for u in range(2):
                re = stage[:ns, u * rows:(u + 1) * rows]
                im = stage[ns:, u * rows:(u + 1) * rows]
                cos, sin = cos_ref[...], sin_ref[...]
                zbuf[pl.ds((s + u) * ns, ns), :] = split_wide(re * cos + im * sin, im * cos - re * sin)
        spec[...] = dot(zbuf[...], fi_ref[...])

    def inverse(left, right, conj, dst, count, base):
        n = rows
        for s in range(8):
            part = pl.ds(s * ns, ns)
            lr, li = left[part, :n], left[part, n:]
            rr, ri = right[part, :n], right[part, n:]
            if conj:
                zbuf[part, :] = split_wide(lr * rr + li * ri, li * rr - lr * ri)
            else:
                zbuf[part, :] = split_wide(lr * rr - li * ri, li * rr + lr * ri)
        full_stage = dot(zbuf[...], bi_ref[...])
        for s in range(0, 8, 2):
            cols = []
            for u in range(2):
                re = full_stage[(s + u) * ns:(s + u + 1) * ns, :n]
                im = full_stage[(s + u) * ns:(s + u + 1) * ns, n:]
                cos, sin = cos_ref[...], sin_ref[...]
                turned = jnp.concatenate([re * cos - im * sin, im * cos + re * sin], axis=0)
                high = turned.astype(BF16)
                low = (turned - high.astype(F32)).astype(BF16)
                cols.append(jnp.concatenate([high, low, high], axis=0))
            back = dot(bo_ref[...], jnp.concatenate(cols, axis=1))
            for u in range(2):
                dst[pl.ds(base + s + u, ns, stride=count), :] = back[:, u * n:(u + 1) * n]

    moved_a.wait_recv()
    wide[...] = recv_a[...].astype(F32).reshape(ns * 16, rows)
    spectra(16, 0, spec_g, 0, 8)
    spectra(16, 8, spec_f, 0, 8)
    inverse(spec_g, spec_f, False, send_b, 8, 0)
    recv_b[pl.ds(pl.multiple_of(me * 8, 8), 8), :] = send_b[pl.ds(pl.multiple_of(me * 8, 8), 8), :]
    moved_b = exchange(send_b, recv_b, 2, True)

    moved_full.wait_recv()
    width = full.shape[2]
    cut = width // (2 * nz)
    for j in range(ny):
        full_t[j] = full[j].T.reshape(nz, 2, cut, rows)
    for step in range(1, group):
        other, device = member(step)
        pltpu.make_async_remote_copy(
            src_ref=full_t.at[other // 2, :, other % 2], dst_ref=grad_recv.at[place],
            send_sem=send_sem.at[5], recv_sem=recv_sem.at[5],
            device_id={"seq": device}, device_id_type=MESH,
        ).start()
    grad_recv[place] = full_t[my_x, :, my_k]
    load.wait()
    gm = jnp.zeros((chans, rows), F32)
    for j in range(ny):
        gm += dot(w_ref[:, j * width:(j + 1) * width], full_t[j].reshape(width, rows))
    gm_t[...] = gm
    send_c[...] = (gm * q_t[...]).astype(BF16).astype(F32)
    recv_c[pl.ds(pl.multiple_of(me * 8, 8), 8), :] = send_c[pl.ds(pl.multiple_of(me * 8, 8), 8), :]
    moved_c = exchange(send_c, recv_c, 3, True)

    moved_b.wait_recv()
    gq_ref[...] = (gm_t[...] * recv_b[...]).T.astype(BF16)
    mixed = (q_t[...] * recv_b[...]).T.astype(BF16)
    mix_send[...] = mixed
    mix_recv[place] = mixed
    for step in range(1, group):
        other, device = member(step)
        pltpu.make_async_remote_copy(
            src_ref=mix_send, dst_ref=mix_recv.at[place],
            send_sem=send_sem.at[6], recv_sem=recv_sem.at[6],
            device_id={"seq": device}, device_id_type=MESH,
        ).start()
    for step in range(1, ny):
        other = lax.rem(my + step, ny)
        columns = pl.ds(pl.multiple_of(other * width, width), width)
        out_send[other] = dot(mix_send[...], w_ref[:, columns]).astype(BF16)
    moved_out = gather_ch(lambda other: out_send.at[other], out_recv, 7)
    out_own[...] = dot(mix_send[...], w_ref[:, pl.ds(pl.multiple_of(my * width, width), width)])

    moved_c.wait_recv()
    wide[pl.ds(0, ns * 8), :] = recv_c[...]
    spectra(8, 0, spec_h, 0, 8)
    inverse(spec_h, spec_f, True, wide, 16, 0)
    inverse(spec_h, spec_g, True, wide, 16, 8)
    send_d[...] = wide[...].reshape(ns, 16, rows).astype(BF16)
    recv_d[me] = send_d[me]
    moved_d = exchange(send_d, recv_d, 4, False)

    def group_wait(send, recv, index):
        return pltpu.make_async_remote_copy(
            src_ref=send, dst_ref=recv, send_sem=send_sem.at[index], recv_sem=recv_sem.at[index],
            device_id={"seq": member(1)[1]}, device_id_type=MESH,
        )

    moved_grad = group_wait(grad_recv.at[pl.ds(0, group - 1)], grad_recv.at[pl.ds(0, group - 1)], 5)
    moved_mix = group_wait(mix_recv.at[pl.ds(0, group - 1)], mix_recv.at[pl.ds(0, group - 1)], 6)
    moved_grad.wait_recv()
    moved_mix.wait_recv()
    columns = jnp.concatenate([grad_recv[i].reshape(nz * cut, rows) for i in range(group)], axis=1)
    part = dot(columns, mix_recv[...].reshape(group * rows, chans))
    part_send[...] = part.astype(BF16).reshape(nz, cut, chans)
    part_recv[my_z] = part_send[my_z]
    for step in range(1, nz):
        other = lax.rem(my_z + step, nz)
        pltpu.make_async_remote_copy(
            src_ref=part_send.at[other], dst_ref=part_recv.at[my_z],
            send_sem=send_sem.at[8], recv_sem=recv_sem.at[8],
            device_id={"seq": (my_x * nz + other) * 2 + my_k}, device_id_type=MESH,
        ).start()
    moved_part = pltpu.make_async_remote_copy(
        src_ref=part_recv.at[pl.ds(0, nz - 1)], dst_ref=part_recv.at[pl.ds(0, nz - 1)],
        send_sem=send_sem.at[8], recv_sem=recv_sem.at[8],
        device_id={"seq": (my_x * nz + lax.rem(my_z + 1, nz)) * 2 + my_k}, device_id_type=MESH,
    )

    moved_out.wait_recv()
    total = out_own[...]
    for step in range(1, ny):
        total += out_recv[lax.rem(my + step, ny)].astype(F32)
    out_ref[...] = total.astype(BF16)

    moved_d.wait_recv()
    back = recv_d[...].astype(F32)
    gg = back[:, :8].reshape(chans, rows).T
    gk_ref[...] = (gg * v_ref[...].astype(F32)).astype(BF16)
    gv_ref[...] = (gg * k_ref[...].astype(F32)).astype(BF16)
    gf_ref[...] = back[:, 8:].reshape(chans, rows).T * scale

    moved_part.wait_recv()
    weight = part_recv[0].astype(F32)
    for i in range(1, nz):
        weight += part_recv[i].astype(F32)
    gw_ref[...] = weight * scale

    for moved in (moved_a, moved_b, moved_c, moved_d, moved_full, moved_out, moved_grad, moved_mix, moved_part):
        moved.wait_send()


def solution(mesh):
    ns, ny = mesh.shape["seq"], mesh.shape["ch"]
    nx, nz, _ = GRID[ns]

    def shards(q, k, v, f, w, g):
        rows, chans = q.shape
        width = g.shape[1]
        cut = width // (2 * nz)
        group = nx * 2
        consts = tables(ns, rows)
        vm = pltpu.VMEM
        sizes = (nx, nz, ns, ny, rows, (ns * rows) ** -0.5)
        tok = lambda dtype: jax.ShapeDtypeStruct((rows, chans), dtype)
        *rest, gw = pl.pallas_call(
            functools.partial(kernel, sizes),
            out_shape=(
                jax.ShapeDtypeStruct((rows, width), BF16), tok(BF16), tok(BF16), tok(BF16), tok(F32),
                jax.ShapeDtypeStruct((cut, chans), F32),
            ),
            in_specs=[pl.BlockSpec(memory_space=pltpu.VMEM)] * 4
            + [pl.BlockSpec(memory_space=pl.ANY)]
            + [pl.BlockSpec(memory_space=pltpu.VMEM)] * 7,
            out_specs=(pl.BlockSpec(memory_space=pltpu.VMEM),) * 6,
            scratch_shapes=[
                vm((2 * ns, 2 * ns), BF16), vm((6 * rows, 2 * rows), BF16),
                vm((6 * rows, 2 * rows), BF16), vm((ns, 6 * ns), BF16),
                vm(w.shape, BF16),
                vm((ns, 16, rows), BF16), vm((ns, 16, rows), BF16),
                vm((chans, rows), F32), vm((chans, rows), F32),
                vm((chans, rows), F32), vm((chans, rows), F32),
                vm((ns, 16, rows), BF16), vm((ns, 16, rows), BF16),
                vm((ns * 16, rows), F32),
                vm((chans, 2 * rows), F32), vm((chans, 2 * rows), F32), vm((chans, 2 * rows), F32),
                vm((chans, 6 * rows), BF16),
                vm((ny, rows, width), BF16), vm((ny, nz, 2, cut, rows), BF16),
                vm((rows, chans), BF16), vm((group, rows, chans), BF16),
                vm((group, nz, cut, rows), BF16),
                vm((nz, cut, chans), BF16), vm((8, 128), F32), vm((nz, cut, chans), BF16),
                vm((ny, rows, width), BF16), vm((ny, rows, width), BF16), vm((rows, width), F32),
                vm((chans, rows), F32), vm((chans, rows), F32),
                pltpu.SemaphoreType.DMA, pltpu.SemaphoreType.DMA((9,)), pltpu.SemaphoreType.DMA((9,)),
            ],
            compiler_params=pltpu.CompilerParams(
                collective_id=0, has_side_effects=True, vmem_limit_bytes=48 * 1024 * 1024
            ),
        )(q, k, v, f, w, g, *consts)
        return (*rest, gw.T)

    tokens = P("seq", "ch")
    return jax.shard_map(
        shards,
        mesh=mesh,
        in_specs=(tokens, tokens, tokens, tokens, P("ch", None), tokens),
        out_specs=(tokens, tokens, tokens, tokens, tokens, P("ch", "seq")),
        check_vma=False,
    )
```

profile of v0, /device:TPU:1, one launch (start us, length us, event | category | flops | bytes accessed | tf_op | source)
XLA Modules:
  0.0 84.2 jit_solution(6260589997194517222)
XLA Ops:
  0.6 0.0 copy-start
  0.6 0.9 %copy-done = bf16[128,1024]{1,0:T(8,128)(2,1)S(1)} copy-done((bf16[128,1024]{1,0:T(8,128)(2,1)S(1)}, bf16[128,1024]{1,0:T(8,128)(2,1)}, u32[]{:S(2)}) %copy-start) | copy-done | bytes 262168
  1.6 0.0 copy-start.1
  1.6 0.9 %copy-done.1 = f32[256,256]{1,0:T(8,128)S(1)} copy-done((f32[256,256]{1,0:T(8,128)S(1)}, f32[256,256]{1,0:T(8,128)}, u32[]{:S(2)}) %copy-start.1) | copy-done | bytes 262168
  2.5 0.0 copy-start.2
  2.5 0.9 %copy-done.2 = f32[256,256]{1,0:T(8,128)S(1)} copy-done((f32[256,256]{1,0:T(8,128)S(1)}, f32[256,256]{1,0:T(8,128)}, u32[]{:S(2)}) %copy-start.2) | copy-done | bytes 262168
  3.5 0.0 copy-start.3
  3.5 0.9 %copy-done.3 = bf16[128,512]{1,0:T(8,128)(2,1)S(1)} copy-done((bf16[128,512]{1,0:T(8,128)(2,1)S(1)}, bf16[128,512]{1,0:T(8,128)(2,1)}, u32[]{:S(2)}) %copy-start.3) | copy-done | bytes 131096
  4.4 0.0 copy-start.4
  4.4 0.9 %copy-done.4 = bf16[128,512]{1,0:T(8,128)(2,1)S(1)} copy-done((bf16[128,512]{1,0:T(8,128)(2,1)S(1)}, bf16[128,512]{1,0:T(8,128)(2,1)}, u32[]{:S(2)}) %copy-start.4) | copy-done | bytes 131096
  5.3 0.0 copy-start.5
  5.3 0.9 %copy-done.5 = bf16[128,512]{1,0:T(8,128)(2,1)S(1)} copy-done((bf16[128,512]{1,0:T(8,128)(2,1)S(1)}, bf16[128,512]{1,0:T(8,128)(2,1)}, u32[]{:S(2)}) %copy-start.5) | copy-done | bytes 131096
  6.2 0.0 copy-start.6
  6.2 0.9 %copy-done.6 = bf16[128,512]{1,0:T(8,128)(2,1)S(1)} copy-done((bf16[128,512]{1,0:T(8,128)(2,1)S(1)}, bf16[128,512]{1,0:T(8,128)(2,1)}, u32[]{:S(2)}) %copy-start.6) | copy-done | bytes 131096
  7.1 0.0 copy-start.7
  7.1 0.8 copy-done.7
  7.9 0.0 copy-start.8
  7.9 0.8 copy-done.8
  8.7 0.0 copy-start.9
  8.7 0.8 copy-done.9
  9.5 0.0 copy-start.10
  9.5 0.8 copy-done.10
  10.2 70.0 %shard_map.163 = (bf16[128,1024]{1,0:T(8,128)(2,1)S(1)}, bf16[128,512]{1,0:T(8,128)(2,1)S(1)}, bf16[128,512]{1,0:T(8,128)(2,1)S(1)}, bf16[128,512]{1,0:T(8,128)(...) custom-call(bf16[128,512]{1,0:T(8,128)(2,1)S(1)} %copy-done.3, bf16[128,512]{1,0:T(8,128)(2,1)S(1)} %copy-done.4, ...), custom_call_target="tpu_custom_call" | custom-call | tf_op jit(solution)/shard_map/pallas_call | solution.py:300
  80.2 0.7 copy.24
  80.9 0.7 copy.25
  81.6 0.7 copy.26
  82.2 0.7 copy.27
  82.9 0.7 copy.28
  83.6 0.7 copy.29
Async XLA Ops:
  0.6 1.0 %copy-start = (bf16[128,1024]{1,0:T(8,128)(2,1)S(1)}, bf16[128,1024]{1,0:T(8,128)(2,1)}, u32[]{:S(2)}) copy-start(bf16[128,1024]{1,0:T(8,128)(2,1)} %go_ref.1) | copy-start | bytes 786436
  1.6 0.9 %copy-start.1 = (f32[256,256]{1,0:T(8,128)S(1)}, f32[256,256]{1,0:T(8,128)}, u32[]{:S(2)}) copy-start(f32[256,256]{1,0:T(8,128)} %constant.14.clone.bi_in) | copy-start | bytes 786436
  2.5 0.9 %copy-start.2 = (f32[256,256]{1,0:T(8,128)S(1)}, f32[256,256]{1,0:T(8,128)}, u32[]{:S(2)}) copy-start(f32[256,256]{1,0:T(8,128)} %constant.13.clone.fi_in) | copy-start | bytes 786436
  3.5 0.9 %copy-start.3 = (bf16[128,512]{1,0:T(8,128)(2,1)S(1)}, bf16[128,512]{1,0:T(8,128)(2,1)}, u32[]{:S(2)}) copy-start(bf16[128,512]{1,0:T(8,128)(2,1)} %q_ref.1) | copy-start | bytes 393220
  4.4 0.9 %copy-start.4 = (bf16[128,512]{1,0:T(8,128)(2,1)S(1)}, bf16[128,512]{1,0:T(8,128)(2,1)}, u32[]{:S(2)}) copy-start(bf16[128,512]{1,0:T(8,128)(2,1)} %k_ref.1) | copy-start | bytes 393220
  5.3 0.9 %copy-start.5 = (bf16[128,512]{1,0:T(8,128)(2,1)S(1)}, bf16[128,512]{1,0:T(8,128)(2,1)}, u32[]{:S(2)}) copy-start(bf16[128,512]{1,0:T(8,128)(2,1)} %v_ref.1) | copy-start | bytes 393220
  6.2 0.9 %copy-start.6 = (bf16[128,512]{1,0:T(8,128)(2,1)S(1)}, bf16[128,512]{1,0:T(8,128)(2,1)}, u32[]{:S(2)}) copy-start(bf16[128,512]{1,0:T(8,128)(2,1)} %f_ref.1) | copy-start | bytes 393220
  7.1 0.8 copy-start.7
  7.9 0.8 copy-start.8
  8.7 0.8 copy-start.9
  9.5 0.8 copy-start.10
where the time goes:
time: 84.7 us; the launch traced here: 84.2 us
  Pallas kernels  70 us (83%)
  local copies, waits for them, and re-layouts  13.6 us (16%)
    pallas_call x1, Pallas kernels, shards(): pl.pallas_call(functools.partial(kernel, sizes), out_shape=(jax.ShapeDtyp...  70 us
    unnamed x28, local copies, waits for them, and re-layouts  13.6 us

commit v1 on v0

v1 whole, which is shorter than its diff:
```python
import functools

import jax
import jax.numpy as jnp
import numpy as np
from jax import lax
from jax.experimental import pallas as pl
from jax.experimental.pallas import tpu as pltpu
from jax.sharding import PartitionSpec as P

F32 = jnp.float32
BF16 = jnp.bfloat16
MESH = pl.DeviceIdType.MESH
GRID = {64: (4, 8, 2), 8: (2, 2, 2)}


def tables(outer, inner, nx, nz):
    length = outer * inner
    i = np.arange(outer)
    j = np.arange(inner)
    first = 2.0 * np.pi * i[:, None] * (i[None, :] + 0.25) / outer
    twist = 2.0 * np.pi * j[None, :] * (i[:, None] + 0.25) / length
    second = 2.0 * np.pi * (j[:, None] * j[None, :] % inner) / inner
    cos, sin = np.cos(second), np.sin(second)
    packed = np.zeros((inner + 5 * outer, 2 * inner))
    packed[:inner] = np.concatenate([cos, sin], 1)
    packed[inner:inner + outer] = np.concatenate([np.cos(twist), np.sin(twist)], 1)
    packed[inner + outer:inner + 3 * outer, :outer] = np.concatenate([np.cos(first).T, -np.sin(first).T], 0)
    back = np.concatenate([np.cos(first), -np.sin(first)], 1) / length
    packed[inner + 3 * outer:inner + 4 * outer, :2 * outer] = back
    packed[inner + 4 * outer:, :2 * outer] = back[i.reshape(nx, nz, 2).transpose(1, 0, 2).reshape(-1)]
    return packed.astype(np.float32)


def halves(table):
    high = table.astype(BF16)
    return high, (table - high.astype(F32)).astype(BF16)


def split_wide(real, imag):
    wide = jnp.concatenate([real, imag], axis=1)
    high = wide.astype(BF16)
    low = (wide - high.astype(F32)).astype(BF16)
    return jnp.concatenate([high, low, high], axis=1)


def dot(a, b):
    return jnp.dot(a, b, preferred_element_type=F32)


def kernel(
    sizes,
    q_hbm, k_hbm, v_hbm, f_hbm, w_hbm, go_hbm, table_hbm,
    out_ref, gq_ref, gk_ref, gv_ref, gf_ref, gw_ref,
    q_ref, k_ref, v_ref, f_ref, go_ref, table,
    fo_ref, fi_ref, bi_ref, bo_ref, bz_ref, w_ref,
    send_a, recv_a, send_b, recv_b, send_c, recv_c, send_d, recv_d,
    wide, spec_g, spec_f, spec_h, zbuf, full, full_t, q_t, q_send, q_recv,
    conv_send, conv_recv, mix_send, mix_recv, grad_recv, part_send, part_recv,
    out_send, out_recv, out_own, gm_t,
    load_sem, send_sem, recv_sem,
):
    nx, nz, ns, ny, rows, scale = sizes
    me = lax.axis_index("seq")
    my = lax.axis_index("ch")
    my_x, my_z, my_k = me // (2 * nz), me // 2 % nz, me % 2
    group = nx * 2
    place = my_x * 2 + my_k
    half = nz // 2
    chans = ns * 8
    width = go_ref.shape[1]
    cut = width // (2 * nz)

    def peer(step):
        return lax.rem(me + step, ns)

    def run_of(device):
        x, z, k = device // (2 * nz), device // 2 % nz, device % 2
        return ((z // half * 2 + k) * nx + x) * half + z % half

    def seq_of(x, z, k):
        return (x * nz + z) * 2 + k

    def remote(src, dst, index, to):
        return pltpu.make_async_remote_copy(
            src_ref=src, dst_ref=dst, send_sem=send_sem.at[index], recv_sem=recv_sem.at[index],
            device_id=to, device_id_type=MESH,
        )

    def nearby(index, ref, count):
        part = ref.at[pl.ds(0, count)]
        return remote(part, part, index, {"seq": peer(1)})

    loads = [
        pltpu.make_async_copy(src, dst, load_sem.at[i])
        for i, (src, dst) in enumerate((
            (k_hbm, k_ref), (v_hbm, v_ref), (f_hbm, f_ref), (go_hbm, go_ref),
            (table_hbm, table), (q_hbm, q_ref), (w_hbm, w_ref),
        ))
    ]
    for load in loads:
        load.start()

    barrier = pltpu.get_barrier_semaphore()

    def greet(step, carry):
        pl.semaphore_signal(barrier, inc=1, device_id={"seq": peer(step)}, device_id_type=MESH)
        return carry

    lax.fori_loop(1, ns, greet, 0)
    for step in range(1, ny):
        pl.semaphore_signal(barrier, inc=1, device_id={"ch": lax.rem(my + step, ny)}, device_id_type=MESH)

    for load in loads[:3]:
        load.wait()
    gated = k_ref[...].astype(F32) * v_ref[...].astype(F32)
    gated_t = gated.T.reshape(ns, 8, rows)
    taps_t = f_ref[...].astype(F32).T.reshape(ns, 8, rows)
    send_a[...] = jnp.concatenate([gated_t, taps_t], axis=1).astype(BF16)
    recv_a[me] = send_a[run_of(me)]
    loads[3].wait()
    pl.semaphore_wait(barrier, ns - 1 + ny - 1)

    def exchange(send, recv, index, where, there):
        def start(step, carry):
            other = peer(step)
            remote(where(send, other), there(recv, me), index, {"seq": other}).start()
            return carry

        lax.fori_loop(1, ns, start, 0)

    def slot(ref, i):
        return ref.at[i]

    def eight(ref, i):
        return ref.at[pl.ds(pl.multiple_of(i * 8, 8), 8)]

    pieces = full.shape[0]
    zs = nz // pieces
    wide_p = width // pieces
    moved_full = []
    moved_grad = []

    def send_piece(p):
        full[p, my] = go_ref[:, p * wide_p:(p + 1) * wide_p]
        for step in (1, ny - 1, *range(2, ny - 1))[:ny - 1]:
            remote(full.at[p, my], full.at[p, my], 1 + p, {"ch": lax.rem(my + step, ny)}).start()
        moved_full.append(nearby(1 + p, full.at[p], ny - 1))

    for p in range(pieces):
        send_piece(p)
    exchange(send_a, recv_a, 0, lambda ref, d: slot(ref, run_of(d)), slot)
    moved_a = nearby(0, recv_a, ns - 1)

    def members():
        for step in range(1, group):
            other = lax.rem(place + step, group)
            yield other, {"seq": seq_of(other // 2, my_z, other % 2)}

    loads[5].wait()
    q_t[...] = q_ref[...].astype(F32).T
    q_send[...] = q_t[...].astype(BF16).reshape(q_send.shape)
    for other, to in members():
        remote(q_send.at[:, other % 2, other // 2], q_recv.at[place], 9, to).start()
    moved_q = nearby(9, q_recv, group - 1)
    q_recv[place] = q_send[:, my_k, my_x]

    def pass_on(p):
        moved_full[p].wait_recv()
        span = pl.ds(p * zs, zs)
        for step in range(ny):
            j = lax.rem(my + step, ny)
            full_t[j, span] = full[p, j].T.reshape(zs, 2, cut, rows)

            @pl.when(j == my_x)
            def _():
                grad_recv[my_k, my_x, span] = full_t[j, span]

            @pl.when(j != my_x)
            def _():
                remote(
                    full_t.at[j, span], grad_recv.at[my_k, my_x, span], 5 + p, {"seq": seq_of(j, my_z, my_k)}
                ).start()
        got = grad_recv.at[0, pl.ds(0, nx - 1), span]
        moved_grad.append(remote(got, got, 5 + p, {"seq": peer(1)}))

    loads[4].wait()
    cos, sin = table[:rows, :rows], table[:rows, rows:]
    high, low = halves(table[rows + ns:rows + 3 * ns, :ns])
    fo_ref[...] = jnp.concatenate([high, low], axis=1)
    high, low = halves(jnp.concatenate([jnp.concatenate([cos, -sin], 1), jnp.concatenate([sin, cos], 1)], 0))
    fi_ref[...] = jnp.concatenate([high, high, low], axis=0)
    high, low = halves(jnp.concatenate([jnp.concatenate([cos, sin], 1), jnp.concatenate([-sin, cos], 1)], 0))
    bi_ref[...] = jnp.concatenate([high, high, low], axis=0)
    high, low = halves(table[rows + 3 * ns:rows + 4 * ns, :2 * ns])
    bo_ref[...] = jnp.concatenate([high, high, low], axis=1)
    high, low = halves(table[rows + 4 * ns:, :2 * ns])
    bz_ref[...] = jnp.concatenate([high, high, low], axis=1)
    turn = pl.ds(rows, ns)

    def spectra(count, base, spec):
        for s in range(0, 8, 2):
            pair = [wide[pl.ds(base + s + u, ns, stride=count), :] for u in range(2)]
            block = jnp.concatenate(pair, axis=1).astype(BF16)
            stage = dot(fo_ref[...], jnp.concatenate([block, block], axis=0))
            for u in range(2):
                re = stage[:ns, u * rows:(u + 1) * rows]
                im = stage[ns:, u * rows:(u + 1) * rows]
                cos, sin = table[turn, :rows], table[turn, rows:]
                zbuf[pl.ds((s + u) * ns, ns), :] = split_wide(re * cos + im * sin, im * cos - re * sin)
        spec[...] = dot(zbuf[...], fi_ref[...])

    def inverse(left, right, conj, last, dst, count, base):
        n = rows
        for s in range(8):
            part = pl.ds(s * ns, ns)
            lr, li = left[part, :n], left[part, n:]
            rr, ri = right[part, :n], right[part, n:]
            if conj:
                zbuf[part, :] = split_wide(lr * rr + li * ri, li * rr - lr * ri)
            else:
                zbuf[part, :] = split_wide(lr * rr - li * ri, li * rr + lr * ri)
        full_stage = dot(zbuf[...], bi_ref[...])
        for s in range(0, 8, 2):
            cols = []
            for u in range(2):
                re = full_stage[(s + u) * ns:(s + u + 1) * ns, :n]
                im = full_stage[(s + u) * ns:(s + u + 1) * ns, n:]
                cos, sin = table[turn, :rows], table[turn, rows:]
                turned = jnp.concatenate([re * cos - im * sin, im * cos + re * sin], axis=0)
                high = turned.astype(BF16)
                low = (turned - high.astype(F32)).astype(BF16)
                cols.append(jnp.concatenate([high, low, high], axis=0))
            back = dot(last[...], jnp.concatenate(cols, axis=1))
            for u in range(2):
                dst[pl.ds(base + s + u, ns, stride=count), :] = back[:, u * n:(u + 1) * n]

    pass_on(0)
    moved_a.wait_recv()
    wide[...] = recv_a[...].astype(F32).reshape(ns * 16, rows)
    spectra(16, 0, spec_g)
    spectra(16, 8, spec_f)
    inverse(spec_g, spec_f, False, bz_ref, send_c, 8, 0)
    send_b[...] = send_c[...].astype(BF16).reshape(nz, group * 8, rows)
    for step in range(1, nz):
        other = lax.rem(my_z + step, nz)
        remote(send_b.at[other], recv_b.at[my_z], 10, {"seq": seq_of(my_x, other, my_k)}).start()
    moved_b = nearby(10, recv_b, nz - 1)
    recv_b[my_z] = send_b[my_z]

    for p in range(1, pieces - 1):
        pass_on(p)

    moved_q.wait_recv()
    moved_b.wait_recv()
    conv = recv_b[...].astype(F32).reshape(nz, group, 8, rows)
    conv = jnp.swapaxes(conv, 0, 1).reshape(group, 2, half * 8, rows)
    mixed = (q_recv[...].astype(F32) * conv).astype(BF16)
    for p in range(2):
        mix_send[p] = mixed[:, p]
        for step in range(1, nx):
            other = lax.rem(my_x + step, nx)
            remote(mix_send.at[p], mix_recv.at[p, my_x], 11 + p, {"seq": seq_of(other, my_z, my_k)}).start()
    conv_send[...] = conv.astype(BF16)
    for other, to in members():
        remote(conv_send.at[other], conv_recv.at[:, my_k, my_x], 13, to).start()
    moved_mix = [nearby(11 + p, mix_recv.at[p], nx - 1) for p in range(2)]
    moved_conv = nearby(13, conv_send, group - 1)
    conv_recv[:, my_k, my_x] = conv_send[place]
    for p in range(2):
        mix_recv[p, my_x] = mix_send[p]

    pass_on(pieces - 1)
    loads[6].wait()
    gm = jnp.zeros((chans, rows), F32)
    for j in range(ny):
        gm += dot(w_ref[:, j * width:(j + 1) * width], full_t[j].reshape(width, rows))
    gm_t[...] = gm
    send_c[...] = (gm * q_t[...]).astype(BF16).astype(F32)
    eight(recv_c, me)[...] = eight(send_c, run_of(me))[...]
    exchange(send_c, recv_c, 14, lambda ref, d: eight(ref, run_of(d)), eight)
    moved_c = nearby(14, recv_c, 8 * (ns - 1))

    moved_conv.wait_recv()
    conv = conv_recv[...].astype(F32).reshape(chans, rows)
    gq_ref[...] = (gm_t[...] * conv).T.astype(BF16)
    mixed = (q_t[...] * conv).T.astype(BF16)
    for step in range(1, ny):
        other = lax.rem(my + step, ny)
        columns = pl.ds(pl.multiple_of(other * width, width), width)
        out_send[other] = dot(mixed, w_ref[:, columns]).astype(BF16)
        remote(out_send.at[other], out_recv.at[my], 15, {"ch": other}).start()
    moved_out = nearby(15, out_recv, ny - 1)
    out_own[...] = dot(mixed, w_ref[:, pl.ds(pl.multiple_of(my * width, width), width)])

    moved_swap = []
    for h in range(2):
        for p in range(h * pieces // 2, (h + 1) * pieces // 2):
            moved_grad[p].wait_recv()
        mine = grad_recv.at[my_k, :, pl.ds(h * half, half)]
        moved_swap.append(remote(mine, mine, 16 + h, {"seq": seq_of(my_x, my_z, 1 - my_k)}))
        moved_swap[h].start()

    moved_part = []
    for p in range(2):
        moved_mix[p].wait_recv()
        if p == 0:
            moved_swap[0].wait_recv()
            moved_swap[1].wait_recv()
        right = jnp.concatenate(
            [mix_recv[p, :, i].reshape(half * 8 * nx, rows) for i in range(group)], axis=1
        )
        for z in range(nz):
            left = jnp.concatenate(
                [grad_recv[i % 2, i // 2, z].reshape(2 * cut, rows) for i in range(group)], axis=1
            )
            part = lax.dot_general(left, right, (((1,), (1,)), ((), ())), preferred_element_type=F32)
            part_send[p, z] = part.astype(BF16).reshape(2, cut, half * 8 * nx)
        for step in range(1, 2 * nz):
            other = lax.rem(my_z * 2 + my_k + step, 2 * nz)
            remote(
                part_send.at[p, other // 2, other % 2], part_recv.at[p, my_z * 2 + my_k], 18 + p,
                {"seq": my_x * 2 * nz + other},
            ).start()
        moved_part.append(nearby(18 + p, part_recv.at[p], 2 * nz - 1))
        part_recv[p, my_z * 2 + my_k] = part_send[p, my_z, my_k]

    moved_c.wait_recv()
    wide[pl.ds(0, ns * 8), :] = recv_c[...]
    spectra(8, 0, spec_h)
    inverse(spec_h, spec_f, True, bo_ref, wide, 16, 0)
    inverse(spec_h, spec_g, True, bo_ref, wide, 16, 8)
    send_d[...] = wide[...].reshape(ns, 16, rows).astype(BF16)
    recv_d[run_of(me)] = send_d[me]
    exchange(send_d, recv_d, 20, slot, lambda ref, d: slot(ref, run_of(d)))
    moved_d = nearby(20, recv_d, ns - 1)

    moved_out.wait_recv()
    total = out_own[...]
    for step in range(1, ny):
        total += out_recv[lax.rem(my + step, ny)].astype(F32)
    out_ref[...] = total.astype(BF16)

    moved_d.wait_recv()
    back = recv_d[...].astype(F32)
    gg = back[:, :8].reshape(chans, rows).T
    gk_ref[...] = (gg * v_ref[...].astype(F32)).astype(BF16)
    gv_ref[...] = (gg * k_ref[...].astype(F32)).astype(BF16)
    gf_ref[...] = back[:, 8:].reshape(chans, rows).T * scale

    for p in range(2):
        moved_part[p].wait_recv()
        for k in range(2):
            weight = part_recv[p, k].astype(F32)
            for i in range(1, nz):
                weight += part_recv[p, 2 * i + k].astype(F32)
            lanes = half * 8 * nx
            gw_ref[:, (2 * p + k) * lanes:(2 * p + k + 1) * lanes] = weight * scale

    for moved in (
        moved_a, moved_b, moved_c, moved_d, moved_q, moved_conv, moved_out,
        *moved_full, *moved_grad, *moved_swap, *moved_mix, *moved_part,
    ):
        moved.wait_send()


def store(*refs):
    count = len(refs) // 2
    copies = [pltpu.make_async_copy(refs[i], refs[count + i], refs[-1].at[i]) for i in range(count)]
    for copy in copies:
        copy.start()
    for copy in copies:
        copy.wait()


def solution(mesh):
    ns, ny = mesh.shape["seq"], mesh.shape["ch"]
    nx, nz, _ = GRID[ns]

    def shards(q, k, v, f, w, g):
        rows, chans = q.shape
        width = g.shape[1]
        cut = width // (2 * nz)
        group = nx * 2
        run = nz * 4
        pieces = min(4, nz)
        table = tables(ns, rows, nx, nz)
        vm = pltpu.VMEM
        sizes = (nx, nz, ns, ny, rows, (ns * rows) ** -0.5)
        tok = lambda dtype: jax.ShapeDtypeStruct((rows, chans), dtype)
        results = pl.pallas_call(
            functools.partial(kernel, sizes),
            out_shape=(
                jax.ShapeDtypeStruct((rows, width), BF16), tok(BF16), tok(BF16), tok(BF16), tok(F32),
                jax.ShapeDtypeStruct((cut, chans), F32),
            ),
            in_specs=[pl.BlockSpec(memory_space=pl.ANY)] * 7,
            out_specs=(pl.BlockSpec(memory_space=pltpu.VMEM),) * 6,
            scratch_shapes=[
                vm(q.shape, BF16), vm(q.shape, BF16), vm(q.shape, BF16), vm(q.shape, BF16),
                vm(g.shape, BF16), vm(table.shape, F32),
                vm((2 * ns, 2 * ns), BF16), vm((6 * rows, 2 * rows), BF16), vm((6 * rows, 2 * rows), BF16),
                vm((ns, 6 * ns), BF16), vm((ns, 6 * ns), BF16), vm(w.shape, BF16),
                vm((ns, 16, rows), BF16), vm((ns, 16, rows), BF16),
                vm((nz, group * 8, rows), BF16), vm((nz, group * 8, rows), BF16),
                vm((chans, rows), F32), vm((chans, rows), F32),
                vm((ns, 16, rows), BF16), vm((ns, 16, rows), BF16),
                vm((ns * 16, rows), F32),
                vm((chans, 2 * rows), F32), vm((chans, 2 * rows), F32), vm((chans, 2 * rows), F32),
                vm((chans, 6 * rows), BF16),
                vm((pieces, ny, rows, width // pieces), BF16), vm((ny, nz, 2, cut, rows), BF16),
                vm((chans, rows), F32),
                vm((2, 2, nx, run, rows), BF16), vm((group, 2, run, rows), BF16),
                vm((group, 2, run, rows), BF16), vm((2, 2, nx, run, rows), BF16),
                vm((2, group, run, rows), BF16), vm((2, nx, group, run, rows), BF16),
                vm((2, nx, nz, 2, cut, rows), BF16),
                vm((2, nz, 2, cut, run * nx), BF16), vm((2, 2 * nz, cut, run * nx), BF16),
                vm((ny, rows, width), BF16), vm((ny, rows, width), BF16), vm((rows, width), F32),
                vm((chans, rows), F32),
                pltpu.SemaphoreType.DMA((7,)), pltpu.SemaphoreType.DMA((21,)), pltpu.SemaphoreType.DMA((21,)),
            ],
            compiler_params=pltpu.CompilerParams(
                collective_id=0, has_side_effects=True, vmem_limit_bytes=56 * 1024 * 1024
            ),
        )(q, k, v, f, w, g, table)
        *rest, gw = pl.pallas_call(
            store,
            out_shape=tuple(jax.ShapeDtypeStruct(r.shape, r.dtype) for r in results),
            in_specs=[pl.BlockSpec(memory_space=pltpu.VMEM)] * 6,
            out_specs=(pl.BlockSpec(memory_space=pl.ANY),) * 6,
            scratch_shapes=[pltpu.SemaphoreType.DMA((6,))],
        )(*results)
        return (*rest, gw.T)

    tokens = P("seq", "ch")
    return jax.shard_map(
        shards,
        mesh=mesh,
        in_specs=(tokens, tokens, tokens, tokens, P("ch", None), tokens),
        out_specs=(tokens, tokens, tokens, tokens, tokens, P("ch", "seq")),
        check_vma=False,
    )
```

time: 84.7 us -> 71.6 us (0.85)
  local copies, waits for them, and re-layouts: 13.6 us -> 0 us
    unnamed x28 -> x0, local copies, waits for them, and re-layouts: 13.6 us -> none
    pallas_call x0 -> x1, Pallas kernels: none -> 2.25 us  [shards(): pl.pallas_call(store, out_shape=tuple((jax.ShapeDtypeStruct(r.shape, r.dt...]
    pallas_call x1, Pallas kernels: 70 us -> 68.6 us  [shards(): pl.pallas_call(functools.partial(kernel, sizes), out_shape=(jax.ShapeDtyp...]
where the time goes in v1:
time: 71.6 us; the launch traced here: 71.4 us
  Pallas kernels  70.8 us (99%)
    pallas_call x1, Pallas kernels, shards(): pl.pallas_call(functools.partial(kernel, sizes), out_shape=(jax.ShapeDtyp...  68.6 us
    pallas_call x1, Pallas kernels, shards(): pl.pallas_call(store, out_shape=tuple((jax.ShapeDtypeStruct(r.shape, r.dt...  2.25 us

profile of v1, /device:TPU:1, one launch (start us, length us, event | category | flops | bytes accessed | tf_op | source)
XLA Modules:
  0.0 71.4 jit_solution(982355879998080868)
XLA Ops:
  0.6 68.6 %shard_map.118 = (bf16[128,1024]{1,0:T(8,128)(2,1)}, bf16[128,512]{1,0:T(8,128)(2,1)}, bf16[128,512]{1,0:T(8,128)(2,1)}, bf16[128,512]{1,0:T(8,128)(2,1)}, f32[128,512]{1,0:T(8,128)}, /*index=5*/f32[64,512]{1,0:T(8,128)}) custom-call(bf16[128,512]{1,0:T(8,128)(2,1)} %q_hbm.1, bf16[128,512]{1,0:T(8,128)(2,1)} %k_hbm.1, bf16[128,512]{1,0:T(8,128)(2,1)} %v_hbm.1, ...), custom_call_target="tpu_custom_call" | custom-call | tf_op jit(solution)/shard_map/pallas_call | solution.py:391
  69.2 2.2 %shard_map.119 = (bf16[128,1024]{1,0:T(8,128)(2,1)}, bf16[128,512]{1,0:T(8,128)(2,1)}, bf16[128,512]{1,0:T(8,128)(2,1)}, bf16[128,512]{1,0:T(8,128)(2,1)}, f32[128,512]{1,0:T(8,128)}, /*index=5*/f32[64,512]{1,0:T(8,128)}) custom-call(bf16[128,1024]{1,0:T(8,128)(2,1)} %get-tuple-element.18.refs_0_, bf16[128,512]{1,0:T(8,128)(2,1)} %get-tuple-element.19.refs_1_, ...), custom_call_target="tpu_custom_call" | custom-call | tf_op jit(solution)/shard_map/pallas_call | solution.py:426

commit v2 on v1

--- a/solution.py
+++ b/solution.py
@@ -11,7 +11,7 @@
 F32 = jnp.float32
 BF16 = jnp.bfloat16
 MESH = pl.DeviceIdType.MESH
-GRID = {64: (4, 8, 2), 8: (2, 2, 2)}
+GRID = {64: (4, 8, 2), 16: (2, 4, 2)}
 
 
 def tables(outer, inner, nx, nz):
@@ -135,14 +135,15 @@
     def eight(ref, i):
         return ref.at[pl.ds(pl.multiple_of(i * 8, 8), 8)]
 
-    pieces = full.shape[0]
-    zs = nz // pieces
-    wide_p = width // pieces
+    pieces = half
+    lows = [*range(0, half, 2), *range(1, half, 2)]
     moved_full = []
     moved_grad = []
 
     def send_piece(p):
-        full[p, my] = go_ref[:, p * wide_p:(p + 1) * wide_p]
+        for u in range(2):
+            first = (u * half + lows[p]) * 2 * cut
+            full[p, my, :, u * 2 * cut:(u + 1) * 2 * cut] = go_ref[:, first:first + 2 * cut]
         for step in (1, ny - 1, *range(2, ny - 1))[:ny - 1]:
             remote(full.at[p, my], full.at[p, my], 1 + p, {"ch": lax.rem(my + step, ny)}).start()
         moved_full.append(nearby(1 + p, full.at[p], ny - 1))
@@ -167,21 +168,21 @@
 
     def pass_on(p):
         moved_full[p].wait_recv()
-        span = pl.ds(p * zs, zs)
+        low = lows[p]
         for step in range(ny):
             j = lax.rem(my + step, ny)
-            full_t[j, span] = full[p, j].T.reshape(zs, 2, cut, rows)
+            full_t[j, :, low] = full[p, j].T.reshape(2, 2, cut, rows)
 
             @pl.when(j == my_x)
             def _():
-                grad_recv[my_k, my_x, span] = full_t[j, span]
+                grad_recv[my_k, my_x, :, low] = full_t[j, :, low]
 
             @pl.when(j != my_x)
             def _():
                 remote(
-                    full_t.at[j, span], grad_recv.at[my_k, my_x, span], 5 + p, {"seq": seq_of(j, my_z, my_k)}
+                    full_t.at[j, :, low], grad_recv.at[my_k, my_x, :, low], 5 + p, {"seq": seq_of(j, my_z, my_k)}
                 ).start()
-        got = grad_recv.at[0, pl.ds(0, nx - 1), span]
+        got = grad_recv.at[0, pl.ds(0, nx - 1), :, low]
         moved_grad.append(remote(got, got, 5 + p, {"seq": peer(1)}))
 
     loads[4].wait()
@@ -256,21 +257,25 @@
     conv = recv_b[...].astype(F32).reshape(nz, group, 8, rows)
     conv = jnp.swapaxes(conv, 0, 1).reshape(group, 2, half * 8, rows)
     mixed = (q_recv[...].astype(F32) * conv).astype(BF16)
-    for p in range(2):
-        mix_send[p] = mixed[:, p]
-        for step in range(1, nx):
-            other = lax.rem(my_x + step, nx)
-            remote(mix_send.at[p], mix_recv.at[p, my_x], 11 + p, {"seq": seq_of(other, my_z, my_k)}).start()
+    mix_send[...] = jnp.swapaxes(mixed, 0, 1)
     conv_send[...] = conv.astype(BF16)
     for other, to in members():
         remote(conv_send.at[other], conv_recv.at[:, my_k, my_x], 13, to).start()
-    moved_mix = [nearby(11 + p, mix_recv.at[p], nx - 1) for p in range(2)]
     moved_conv = nearby(13, conv_send, group - 1)
     conv_recv[:, my_k, my_x] = conv_send[place]
-    for p in range(2):
-        mix_recv[p, my_x] = mix_send[p]
 
     pass_on(pieces - 1)
+
+    def swap(h):
+        for p in range(h * half // 2, (h + 1) * half // 2):
+            moved_grad[p].wait_recv()
+            mine = grad_recv.at[my_k, :, :, lows[p]]
+            remote(mine, mine, 16 + h, {"seq": seq_of(my_x, my_z, 1 - my_k)}).start()
+        both = grad_recv.at[0, :, :, pl.ds(0, half // 2)]
+        return remote(both, both, 16 + h, {"seq": peer(1)})
+
+    moved_swap = [swap(0)]
+
     loads[6].wait()
     gm = jnp.zeros((chans, rows), F32)
     for j in range(ny):
@@ -280,6 +285,13 @@
     eight(recv_c, me)[...] = eight(send_c, run_of(me))[...]
     exchange(send_c, recv_c, 14, lambda ref, d: eight(ref, run_of(d)), eight)
     moved_c = nearby(14, recv_c, 8 * (ns - 1))
+
+    for step in range(1, nx):
+        other = lax.rem(my_x + step, nx)
+        remote(mix_send, mix_recv.at[my_x], 11, {"seq": seq_of(other, my_z, my_k)}).start()
+    moved_mix = nearby(11, mix_recv, nx - 1)
+    mix_recv[my_x] = mix_send[...]
+    moved_swap.append(swap(1))
 
     moved_conv.wait_recv()
     conv = conv_recv[...].astype(F32).reshape(chans, rows)
@@ -293,38 +305,6 @@
     moved_out = nearby(15, out_recv, ny - 1)
     out_own[...] = dot(mixed, w_ref[:, pl.ds(pl.multiple_of(my * width, width), width)])
 
-    moved_swap = []
-    for h in range(2):
-        for p in range(h * pieces // 2, (h + 1) * pieces // 2):
-            moved_grad[p].wait_recv()
-        mine = grad_recv.at[my_k, :, pl.ds(h * half, half)]
-        moved_swap.append(remote(mine, mine, 16 + h, {"seq": seq_of(my_x, my_z, 1 - my_k)}))
-        moved_swap[h].start()
-
-    moved_part = []
-    for p in range(2):
-        moved_mix[p].wait_recv()
-        if p == 0:
-            moved_swap[0].wait_recv()
-            moved_swap[1].wait_recv()
-        right = jnp.concatenate(
-            [mix_recv[p, :, i].reshape(half * 8 * nx, rows) for i in range(group)], axis=1
-        )
-        for z in range(nz):
-            left = jnp.concatenate(
-                [grad_recv[i % 2, i // 2, z].reshape(2 * cut, rows) for i in range(group)], axis=1
-            )
-            part = lax.dot_general(left, right, (((1,), (1,)), ((), ())), preferred_element_type=F32)
-            part_send[p, z] = part.astype(BF16).reshape(2, cut, half * 8 * nx)
-        for step in range(1, 2 * nz):
-            other = lax.rem(my_z * 2 + my_k + step, 2 * nz)
-            remote(
-                part_send.at[p, other // 2, other % 2], part_recv.at[p, my_z * 2 + my_k], 18 + p,
-                {"seq": my_x * 2 * nz + other},
-            ).start()
-        moved_part.append(nearby(18 + p, part_recv.at[p], 2 * nz - 1))
-        part_recv[p, my_z * 2 + my_k] = part_send[p, my_z, my_k]
-
     moved_c.wait_recv()
     wide[pl.ds(0, ns * 8), :] = recv_c[...]
     spectra(8, 0, spec_h)
@@ -335,6 +315,35 @@
     exchange(send_d, recv_d, 20, slot, lambda ref, d: slot(ref, run_of(d)))
     moved_d = nearby(20, recv_d, ns - 1)
 
+    moved_mix.wait_recv()
+    right = jnp.concatenate(
+        [mix_recv[:, p, i].reshape(half * 8 * nx, rows) for p in range(2) for i in range(group)], axis=1
+    )
+    right = jnp.concatenate([right[:, :group * rows], right[:, group * rows:]], axis=0)
+    here = my_z * 2 + my_k
+    for h in range(2):
+        moved_swap[h].wait_recv()
+        for t in range(half):
+            z = lax.rem(2 * (my_z // 2 + t), nz) + h
+            left = jnp.concatenate(
+                [grad_recv[i % 2, i // 2, z // half, z % half].reshape(2 * cut, rows) for i in range(group)], axis=1
+            )
+            part = lax.dot_general(left, right, (((1,), (1,)), ((), ())), preferred_element_type=F32)
+            part_send[z] = part.astype(BF16).reshape(2, cut, half * 16 * nx)
+            for k in range(2):
+                there = z * 2 + k
+
+                @pl.when(there == here)
+                def _():
+                    part_recv[here] = part_send[z, k]
+
+                @pl.when(there != here)
+                def _():
+                    remote(
+                        part_send.at[z, k], part_recv.at[here], 18, {"seq": my_x * 2 * nz + there}
+                    ).start()
+    moved_part = nearby(18, part_recv, 2 * nz - 1)
+
     moved_out.wait_recv()
     total = out_own[...]
     for step in range(1, ny):
@@ -348,18 +357,18 @@
     gv_ref[...] = (gg * k_ref[...].astype(F32)).astype(BF16)
     gf_ref[...] = back[:, 8:].reshape(chans, rows).T * scale
 
-    for p in range(2):
-        moved_part[p].wait_recv()
-        for k in range(2):
-            weight = part_recv[p, k].astype(F32)
-            for i in range(1, nz):
-                weight += part_recv[p, 2 * i + k].astype(F32)
-            lanes = half * 8 * nx
-            gw_ref[:, (2 * p + k) * lanes:(2 * p + k + 1) * lanes] = weight * scale
+    moved_part.wait_recv()
+    lanes = half * 8 * nx
+    for k in range(2):
+        weight = part_recv[k].astype(F32)
+        for i in range(1, nz):
+            weight += part_recv[2 * i + k].astype(F32)
+        for p in range(2):
+            gw_ref[:, (2 * p + k) * lanes:(2 * p + k + 1) * lanes] = weight[:, p * lanes:(p + 1) * lanes] * scale
 
     for moved in (
         moved_a, moved_b, moved_c, moved_d, moved_q, moved_conv, moved_out,
-        *moved_full, *moved_grad, *moved_swap, *moved_mix, *moved_part,
+        *moved_full, moved_mix, moved_part, *moved_grad, *moved_swap,
     ):
         moved.wait_send()
 
@@ -383,7 +392,7 @@
         cut = width // (2 * nz)
         group = nx * 2
         run = nz * 4
-        pieces = min(4, nz)
+        pieces = nz // 2
         table = tables(ns, rows, nx, nz)
         vm = pltpu.VMEM
         sizes = (nx, nz, ns, ny, rows, (ns * rows) ** -0.5)
@@ -408,13 +417,13 @@
                 vm((ns * 16, rows), F32),
                 vm((chans, 2 * rows), F32), vm((chans, 2 * rows), F32), vm((chans, 2 * rows), F32),
                 vm((chans, 6 * rows), BF16),
-                vm((pieces, ny, rows, width // pieces), BF16), vm((ny, nz, 2, cut, rows), BF16),
+                vm((pieces, ny, rows, width // pieces), BF16), vm((ny, 2, nz // 2, 2, cut, rows), BF16),
                 vm((chans, rows), F32),
                 vm((2, 2, nx, run, rows), BF16), vm((group, 2, run, rows), BF16),
                 vm((group, 2, run, rows), BF16), vm((2, 2, nx, run, rows), BF16),
-                vm((2, group, run, rows), BF16), vm((2, nx, group, run, rows), BF16),
-                vm((2, nx, nz, 2, cut, rows), BF16),
-                vm((2, nz, 2, cut, run * nx), BF16), vm((2, 2 * nz, cut, run * nx), BF16),
+                vm((2, group, run, rows), BF16), vm((nx, 2, group, run, rows), BF16),
+                vm((2, nx, 2, nz // 2, 2, cut, rows), BF16),
+                vm((nz, 2, cut, 2 * run * nx), BF16), vm((2 * nz, cut, 2 * run * nx), BF16),
                 vm((ny, rows, width), BF16), vm((ny, rows, width), BF16), vm((rows, width), F32),
                 vm((chans, rows), F32),
                 pltpu.SemaphoreType.DMA((7,)), pltpu.SemaphoreType.DMA((21,)), pltpu.SemaphoreType.DMA((21,)),

time: 71.6 us -> 65.9 us (0.920)
  Pallas kernels: 70.8 us -> 64.7 us
    pallas_call x1, Pallas kernels: 68.6 us -> 62.4 us  [shards(): pl.pallas_call(functools.partial(kernel, sizes), out_shape=(jax.ShapeDtyp...]
where the time goes in v2:
time: 65.9 us; the launch traced here: 65.3 us
  Pallas kernels  64.7 us (98%)
    pallas_call x1, Pallas kernels, shards(): pl.pallas_call(functools.partial(kernel, sizes), out_shape=(jax.ShapeDtyp...  62.4 us
    pallas_call x1, Pallas kernels, shards(): pl.pallas_call(store, out_shape=tuple((jax.ShapeDtypeStruct(r.shape, r.dt...  2.25 us

profile of v2, /device:TPU:1, one launch (start us, length us, event | category | flops | bytes accessed | tf_op | source)
XLA Modules:
  0.0 65.3 jit_solution(3952086658002008758)
XLA Ops:
  0.6 62.4 %shard_map.118 = (bf16[128,1024]{1,0:T(8,128)(2,1)}, bf16[128,512]{1,0:T(8,128)(2,1)}, bf16[128,512]{1,0:T(8,128)(2,1)}, bf16[128,512]{1,0:T(8,128)(2,1)}, f32[128,512]{1,0:T(8,128)}, /*index=5*/f32[64,512]{1,0:T(8,128)}) custom-call(bf16[128,512]{1,0:T(8,128)(2,1)} %q_hbm.1, bf16[128,512]{1,0:T(8,128)(2,1)} %k_hbm.1, bf16[128,512]{1,0:T(8,128)(2,1)} %v_hbm.1, ...), custom_call_target="tpu_custom_call" | custom-call | tf_op jit(solution)/shard_map/pallas_call | solution.py:400
  63.1 2.2 %shard_map.119 = (bf16[128,1024]{1,0:T(8,128)(2,1)}, bf16[128,512]{1,0:T(8,128)(2,1)}, bf16[128,512]{1,0:T(8,128)(2,1)}, bf16[128,512]{1,0:T(8,128)(2,1)}, f32[128,512]{1,0:T(8,128)}, /*index=5*/f32[64,512]{1,0:T(8,128)}) custom-call(bf16[128,1024]{1,0:T(8,128)(2,1)} %get-tuple-element.18.refs_0_, bf16[128,512]{1,0:T(8,128)(2,1)} %get-tuple-element.19.refs_1_, ...), custom_call_target="tpu_custom_call" | custom-call | tf_op jit(solution)/shard_map/pallas_call | solution.py:435

commit v3 on v2

--- a/solution.py
+++ b/solution.py
@@ -72,7 +72,7 @@
     cut = width // (2 * nz)
 
     def peer(step):
-        return lax.rem(me + step, ns)
+        return lax.rem(me + step * 53, ns)
 
     def run_of(device):
         x, z, k = device // (2 * nz), device // 2 % nz, device % 2
@@ -166,22 +166,19 @@
     moved_q = nearby(9, q_recv, group - 1)
     q_recv[place] = q_send[:, my_k, my_x]
 
+    def turn_over(p):
+        moved_full[p].wait_recv()
+        for j in range(ny):
+            full_t[j, :, lows[p]] = full[p, j].T.reshape(2, 2, cut, rows)
+
     def pass_on(p):
-        moved_full[p].wait_recv()
         low = lows[p]
-        for step in range(ny):
-            j = lax.rem(my + step, ny)
-            full_t[j, :, low] = full[p, j].T.reshape(2, 2, cut, rows)
-
-            @pl.when(j == my_x)
-            def _():
-                grad_recv[my_k, my_x, :, low] = full_t[j, :, low]
-
-            @pl.when(j != my_x)
-            def _():
-                remote(
-                    full_t.at[j, :, low], grad_recv.at[my_k, my_x, :, low], 5 + p, {"seq": seq_of(j, my_z, my_k)}
-                ).start()
+        for step in range(1, nx):
+            j = lax.rem(my_x + step, nx)
+            remote(
+                full_t.at[j, :, low], grad_recv.at[my_k, my_x, :, low], 5 + p, {"seq": seq_of(j, my_z, my_k)}
+            ).start()
+        grad_recv[my_k, my_x, :, low] = full_t[my_x, :, low]
         got = grad_recv.at[0, pl.ds(0, nx - 1), :, low]
         moved_grad.append(remote(got, got, 5 + p, {"seq": peer(1)}))
 
@@ -199,9 +196,9 @@
     bz_ref[...] = jnp.concatenate([high, high, low], axis=1)
     turn = pl.ds(rows, ns)
 
-    def spectra(count, base, spec):
+    def spectra(src, count, base, spec):
         for s in range(0, 8, 2):
-            pair = [wide[pl.ds(base + s + u, ns, stride=count), :] for u in range(2)]
+            pair = [src[pl.ds(base + s + u, ns, stride=count), :] for u in range(2)]
             block = jnp.concatenate(pair, axis=1).astype(BF16)
             stage = dot(fo_ref[...], jnp.concatenate([block, block], axis=0))
             for u in range(2):
@@ -236,11 +233,12 @@
             for u in range(2):
                 dst[pl.ds(base + s + u, ns, stride=count), :] = back[:, u * n:(u + 1) * n]
 
+    turn_over(0)
     pass_on(0)
     moved_a.wait_recv()
     wide[...] = recv_a[...].astype(F32).reshape(ns * 16, rows)
-    spectra(16, 0, spec_g)
-    spectra(16, 8, spec_f)
+    spectra(wide, 16, 0, spec_g)
+    spectra(wide, 16, 8, spec_f)
     inverse(spec_g, spec_f, False, bz_ref, send_c, 8, 0)
     send_b[...] = send_c[...].astype(BF16).reshape(nz, group * 8, rows)
     for step in range(1, nz):
@@ -249,8 +247,21 @@
     moved_b = nearby(10, recv_b, nz - 1)
     recv_b[my_z] = send_b[my_z]
 
+    loads[6].wait()
+
+    def add_up(p):
+        total = jnp.zeros((chans, rows), F32) if p == 0 else gm_t[...]
+        for j in range(ny):
+            first = [j * width + (u * half + lows[p]) * 2 * cut for u in range(2)]
+            weights = jnp.concatenate([w_ref[:, i:i + 2 * cut] for i in first], axis=1)
+            total += dot(weights, full_t[j, :, lows[p]].reshape(4 * cut, rows))
+        gm_t[...] = total
+
+    add_up(0)
     for p in range(1, pieces - 1):
+        turn_over(p)
         pass_on(p)
+        add_up(p)
 
     moved_q.wait_recv()
     moved_b.wait_recv()
@@ -264,8 +275,20 @@
     moved_conv = nearby(13, conv_send, group - 1)
     conv_recv[:, my_k, my_x] = conv_send[place]
 
+    turn_over(pieces - 1)
     pass_on(pieces - 1)
-
+    add_up(pieces - 1)
+
+    send_c[...] = (gm_t[...] * q_t[...]).astype(BF16).astype(F32)
+    eight(recv_c, me)[...] = eight(send_c, run_of(me))[...]
+    exchange(send_c, recv_c, 14, lambda ref, d: eight(ref, run_of(d)), eight)
+    moved_c = nearby(14, recv_c, 8 * (ns - 1))
+
+    for step in range(1, nx):
+        other = lax.rem(my_x + step, nx)
+        remote(mix_send, mix_recv.at[my_x], 11, {"seq": seq_of(other, my_z, my_k)}).start()
+    moved_mix = nearby(11, mix_recv, nx - 1)
+    mix_recv[my_x] = mix_send[...]
     def swap(h):
         for p in range(h * half // 2, (h + 1) * half // 2):
             moved_grad[p].wait_recv()
@@ -274,24 +297,8 @@
         both = grad_recv.at[0, :, :, pl.ds(0, half // 2)]
         return remote(both, both, 16 + h, {"seq": peer(1)})
 
-    moved_swap = [swap(0)]
-
-    loads[6].wait()
-    gm = jnp.zeros((chans, rows), F32)
-    for j in range(ny):
-        gm += dot(w_ref[:, j * width:(j + 1) * width], full_t[j].reshape(width, rows))
-    gm_t[...] = gm
-    send_c[...] = (gm * q_t[...]).astype(BF16).astype(F32)
-    eight(recv_c, me)[...] = eight(send_c, run_of(me))[...]
-    exchange(send_c, recv_c, 14, lambda ref, d: eight(ref, run_of(d)), eight)
-    moved_c = nearby(14, recv_c, 8 * (ns - 1))
-
-    for step in range(1, nx):
-        other = lax.rem(my_x + step, nx)
-        remote(mix_send, mix_recv.at[my_x], 11, {"seq": seq_of(other, my_z, my_k)}).start()
-    moved_mix = nearby(11, mix_recv, nx - 1)
-    mix_recv[my_x] = mix_send[...]
-    moved_swap.append(swap(1))
+    moved_swap = [swap(0), swap(1)]
+
 
     moved_conv.wait_recv()
     conv = conv_recv[...].astype(F32).reshape(chans, rows)
@@ -306,8 +313,7 @@
     out_own[...] = dot(mixed, w_ref[:, pl.ds(pl.multiple_of(my * width, width), width)])
 
     moved_c.wait_recv()
-    wide[pl.ds(0, ns * 8), :] = recv_c[...]
-    spectra(8, 0, spec_h)
+    spectra(recv_c, 8, 0, spec_h)
     inverse(spec_h, spec_f, True, bo_ref, wide, 16, 0)
     inverse(spec_h, spec_g, True, bo_ref, wide, 16, 8)
     send_d[...] = wide[...].reshape(ns, 16, rows).astype(BF16)
@@ -323,7 +329,7 @@
     here = my_z * 2 + my_k
     for h in range(2):
         moved_swap[h].wait_recv()
-        for t in range(half):
+        for t in (half // 2, *(i for i in range(1, half) if i != half // 2), 0):
             z = lax.rem(2 * (my_z // 2 + t), nz) + h
             left = jnp.concatenate(
                 [grad_recv[i % 2, i // 2, z // half, z % half].reshape(2 * cut, rows) for i in range(group)], axis=1

time: 65.9 us -> 64.4 us (0.977)
  Pallas kernels: 64.7 us -> 63.6 us
    pallas_call x1, Pallas kernels: 62.4 us -> 61.4 us  [shards(): pl.pallas_call(functools.partial(kernel, sizes), out_shape=(jax.ShapeDtyp...]
where the time goes in v3:
time: 64.4 us; the launch traced here: 64.3 us
  Pallas kernels  63.6 us (99%)
    pallas_call x1, Pallas kernels, shards(): pl.pallas_call(functools.partial(kernel, sizes), out_shape=(jax.ShapeDtyp...  61.4 us
    pallas_call x1, Pallas kernels, shards(): pl.pallas_call(store, out_shape=tuple((jax.ShapeDtypeStruct(r.shape, r.dt...  2.25 us

profile of v3, /device:TPU:1, one launch (start us, length us, event | category | flops | bytes accessed | tf_op | source)
XLA Modules:
  0.0 64.3 jit_solution(15685933747058260111)
XLA Ops:
  0.6 61.4 %shard_map.118 = (bf16[128,1024]{1,0:T(8,128)(2,1)}, bf16[128,512]{1,0:T(8,128)(2,1)}, bf16[128,512]{1,0:T(8,128)(2,1)}, bf16[128,512]{1,0:T(8,128)(2,1)}, f32[128,512]{1,0:T(8,128)}, /*index=5*/f32[64,512]{1,0:T(8,128)}) custom-call(bf16[128,512]{1,0:T(8,128)(2,1)} %q_hbm.1, bf16[128,512]{1,0:T(8,128)(2,1)} %k_hbm.1, bf16[128,512]{1,0:T(8,128)(2,1)} %v_hbm.1, ...), custom_call_target="tpu_custom_call" | custom-call | tf_op jit(solution)/shard_map/pallas_call | solution.py:406
  62.0 2.2 %shard_map.119 = (bf16[128,1024]{1,0:T(8,128)(2,1)}, bf16[128,512]{1,0:T(8,128)(2,1)}, bf16[128,512]{1,0:T(8,128)(2,1)}, bf16[128,512]{1,0:T(8,128)(2,1)}, f32[128,512]{1,0:T(8,128)}, /*index=5*/f32[64,512]{1,0:T(8,128)}) custom-call(bf16[128,1024]{1,0:T(8,128)(2,1)} %get-tuple-element.18.refs_0_, bf16[128,512]{1,0:T(8,128)(2,1)} %get-tuple-element.19.refs_1_, ...), custom_call_target="tpu_custom_call" | custom-call | tf_op jit(solution)/shard_map/pallas_call | solution.py:441

commit v4 on v3

--- a/solution.py
+++ b/solution.py
@@ -54,7 +54,7 @@
     out_ref, gq_ref, gk_ref, gv_ref, gf_ref, gw_ref,
     q_ref, k_ref, v_ref, f_ref, go_ref, table,
     fo_ref, fi_ref, bi_ref, bo_ref, bz_ref, w_ref,
-    send_a, recv_a, send_b, recv_b, send_c, recv_c, send_d, recv_d,
+    send_a, recv_a, send_b, recv_b, stage_c, send_c, recv_c, give_c, take_c, send_d, recv_d,
     wide, spec_g, spec_f, spec_h, zbuf, full, full_t, q_t, q_send, q_recv,
     conv_send, conv_recv, mix_send, mix_recv, grad_recv, part_send, part_recv,
     out_send, out_recv, out_own, gm_t,
@@ -131,9 +131,6 @@
 
     def slot(ref, i):
         return ref.at[i]
-
-    def eight(ref, i):
-        return ref.at[pl.ds(pl.multiple_of(i * 8, 8), 8)]
 
     pieces = half
     lows = [*range(0, half, 2), *range(1, half, 2)]
@@ -239,8 +236,8 @@
     wide[...] = recv_a[...].astype(F32).reshape(ns * 16, rows)
     spectra(wide, 16, 0, spec_g)
     spectra(wide, 16, 8, spec_f)
-    inverse(spec_g, spec_f, False, bz_ref, send_c, 8, 0)
-    send_b[...] = send_c[...].astype(BF16).reshape(nz, group * 8, rows)
+    inverse(spec_g, spec_f, False, bz_ref, stage_c, 8, 0)
+    send_b[...] = stage_c[...].astype(BF16).reshape(nz, group * 8, rows)
     for step in range(1, nz):
         other = lax.rem(my_z + step, nz)
         remote(send_b.at[other], recv_b.at[my_z], 10, {"seq": seq_of(my_x, other, my_k)}).start()
@@ -279,10 +276,18 @@
     pass_on(pieces - 1)
     add_up(pieces - 1)
 
-    send_c[...] = (gm_t[...] * q_t[...]).astype(BF16).astype(F32)
-    eight(recv_c, me)[...] = eight(send_c, run_of(me))[...]
-    exchange(send_c, recv_c, 14, lambda ref, d: eight(ref, run_of(d)), eight)
-    moved_c = nearby(14, recv_c, 8 * (ns - 1))
+    grad_conv = (gm_t[...] * q_t[...]).reshape(2, 2, nx, half, 8, rows)
+    send_c[...] = jnp.transpose(grad_conv, (2, 0, 3, 1, 4, 5)).reshape(ns // 2, 16, rows).astype(BF16)
+    chip = me // 2
+
+    def start_c(step, carry):
+        other = lax.rem(chip + step * 11, ns // 2)
+        remote(send_c.at[other], recv_c.at[chip], 14, {"seq": other * 2 + my_k}).start()
+        return carry
+
+    lax.fori_loop(1, ns // 2, start_c, 0)
+    recv_c[chip] = send_c[chip]
+    moved_c = nearby(14, recv_c, ns // 2 - 1)
 
     for step in range(1, nx):
         other = lax.rem(my_x + step, nx)
@@ -313,7 +318,17 @@
     out_own[...] = dot(mixed, w_ref[:, pl.ds(pl.multiple_of(my * width, width), width)])
 
     moved_c.wait_recv()
-    spectra(recv_c, 8, 0, spec_h)
+    got = recv_c[...].astype(F32)
+    keep = jnp.where(my_k == 0, got[:, :8], got[:, 8:])
+    give = jnp.where(my_k == 0, got[:, 8:], got[:, :8])
+    give_c[...] = give.reshape(ns // 4, 16, rows).astype(BF16)
+    moved_give = remote(give_c, take_c, 12, {"seq": seq_of(my_x, my_z, 1 - my_k)})
+    moved_give.start()
+    moved_give.wait_recv()
+    take = take_c[...].astype(F32).reshape(ns // 2, 8, rows)
+    both = [jnp.where(my_k == 0, keep, take), jnp.where(my_k == 0, take, keep)]
+    wide[pl.ds(0, ns * 8), :] = jnp.stack(both, axis=1).reshape(ns * 8, rows)
+    spectra(wide, 8, 0, spec_h)
     inverse(spec_h, spec_f, True, bo_ref, wide, 16, 0)
     inverse(spec_h, spec_g, True, bo_ref, wide, 16, 8)
     send_d[...] = wide[...].reshape(ns, 16, rows).astype(BF16)
@@ -373,7 +388,7 @@
             gw_ref[:, (2 * p + k) * lanes:(2 * p + k + 1) * lanes] = weight[:, p * lanes:(p + 1) * lanes] * scale
 
     for moved in (
-        moved_a, moved_b, moved_c, moved_d, moved_q, moved_conv, moved_out,
+        moved_a, moved_b, moved_c, moved_give, moved_d, moved_q, moved_conv, moved_out,
         *moved_full, moved_mix, moved_part, *moved_grad, *moved_swap,
     ):
         moved.wait_send()
@@ -418,7 +433,8 @@
                 vm((ns, 6 * ns), BF16), vm((ns, 6 * ns), BF16), vm(w.shape, BF16),
                 vm((ns, 16, rows), BF16), vm((ns, 16, rows), BF16),
                 vm((nz, group * 8, rows), BF16), vm((nz, group * 8, rows), BF16),
-                vm((chans, rows), F32), vm((chans, rows), F32),
+                vm((chans, rows), F32), vm((ns // 2, 16, rows), BF16), vm((ns // 2, 16, rows), BF16),
+                vm((ns // 4, 16, rows), BF16), vm((ns // 4, 16, rows), BF16),
                 vm((ns, 16, rows), BF16), vm((ns, 16, rows), BF16),
                 vm((ns * 16, rows), F32),
                 vm((chans, 2 * rows), F32), vm((chans, 2 * rows), F32), vm((chans, 2 * rows), F32),

time: 64.4 us -> 64.9 us (level)
  no operation moved by 1% of the time
where the time goes in v4:
time: 64.9 us; the launch traced here: 64.8 us
  Pallas kernels  64.1 us (99%)
    pallas_call x1, Pallas kernels, shards(): pl.pallas_call(functools.partial(kernel, sizes), out_shape=(jax.ShapeDtyp...  61.9 us
    pallas_call x1, Pallas kernels, shards(): pl.pallas_call(store, out_shape=tuple((jax.ShapeDtypeStruct(r.shape, r.dt...  2.25 us

profile of v4, /device:TPU:1, one launch (start us, length us, event | category | flops | bytes accessed | tf_op | source)
XLA Modules:
  0.0 64.8 jit_solution(17924896420986337433)
XLA Ops:
  0.6 61.9 %shard_map.118 = (bf16[128,1024]{1,0:T(8,128)(2,1)}, bf16[128,512]{1,0:T(8,128)(2,1)}, bf16[128,512]{1,0:T(8,128)(2,1)}, bf16[128,512]{1,0:T(8,128)(2,1)}, f32[128,512]{1,0:T(8,128)}, /*index=5*/f32[64,512]{1,0:T(8,128)}) custom-call(bf16[128,512]{1,0:T(8,128)(2,1)} %q_hbm.1, bf16[128,512]{1,0:T(8,128)(2,1)} %k_hbm.1, bf16[128,512]{1,0:T(8,128)(2,1)} %v_hbm.1, ...), custom_call_target="tpu_custom_call" | custom-call | tf_op jit(solution)/shard_map/pallas_call | solution.py:421
  62.5 2.2 %shard_map.119 = (bf16[128,1024]{1,0:T(8,128)(2,1)}, bf16[128,512]{1,0:T(8,128)(2,1)}, bf16[128,512]{1,0:T(8,128)(2,1)}, bf16[128,512]{1,0:T(8,128)(2,1)}, f32[128,512]{1,0:T(8,128)}, /*index=5*/f32[64,512]{1,0:T(8,128)}) custom-call(bf16[128,1024]{1,0:T(8,128)(2,1)} %get-tuple-element.18.refs_0_, bf16[128,512]{1,0:T(8,128)(2,1)} %get-tuple-element.19.refs_1_, ...), custom_call_target="tpu_custom_call" | custom-call | tf_op jit(solution)/shard_map/pallas_call | solution.py:457
